TPU v7x, 32 devices: a whole 2x2x4 slice. The times are simulated.
32 devices in a mesh: dp: 2 (over x), expert: 8 (over z, core), tensor: 2 (over y).
Axes of the slice: x: 2, y: 2, z: 4, core: 2. Of those that a mesh axis runs over, the one named last changes fastest.
Arguments:
- tokens: bfloat16 [256, 2048], P(('dp', 'expert')), may hold values from -6 to 6
- routes: int32 [256, 8], P(('dp', 'expert')), may hold values from 0 to 15, all different within a row; in each aligned block of 16 rows (0 to 15, 16 to 31, ...) at most 16 rows name the same one
- route_weight: float32 [256, 8], P(('dp', 'expert')), may hold values from 0.02 to 0.5
- weights_gate_up: bfloat16 [16, 2048, 2, 768], P('expert', None, None, 'tensor'), may hold values from -0.125 to 0.125
- weights_down: bfloat16 [16, 2048, 768], P('expert', None, 'tensor'), may hold values from -0.21875 to 0.21875
- cotangent: bfloat16 [256, 2048], P(('dp', 'expert')), may hold values from -6 to 6
Outputs:
- layer_out: bfloat16 [256, 2048], P(('dp', 'expert'), 'tensor')
- tokens_grad: bfloat16 [256, 2048], P(('dp', 'expert'), 'tensor')
- gate_up_grad: bfloat16 [16, 2048, 2, 768], P('expert', 'dp', None, 'tensor')
- down_grad: bfloat16 [16, 2048, 768], P('expert', 'dp', 'tensor')
Inputs may be any that keep to these rules, and one draw needn't show every extreme that they name: `routes`: each row names 8 different experts. Among the 16 rows of one index of dp and expert no expert is named more than 16 times, a bound that some block reaches.
All inputs are finite; a program needn't handle non-finite values.
Results may differ from a plain program's by a relative error of at most 0.0072.
Values may be sent and summed in bfloat16 or wider, within the bound.
A program may use at most 64 MiB of HBM per device.

v0:
```python
import jax
import jax.numpy as jnp
from jax import lax
from jax.sharding import PartitionSpec as P

F32 = jnp.float32
BF16 = jnp.bfloat16


def cut(value):
    return lax.reduce_precision(value, exponent_bits=8, mantissa_bits=7)


def body(tokens, routes, route_weight, weights_gate_up, weights_down, cotangent):
    tok_rows, width = tokens.shape
    expert_local = weights_gate_up.shape[0]
    n_expert = lax.axis_size("expert")
    n_tensor = lax.axis_size("tensor")
    n_dp = lax.axis_size("dp")
    expert_total = expert_local * n_expert
    group = tok_rows * n_expert
    my_dp = lax.axis_index("dp")
    chosen = routes[:, :, None] == jnp.arange(expert_total, dtype=jnp.int32)[None, None, :]
    dense = jnp.sum(jnp.where(chosen, route_weight[:, :, None], 0.0), axis=1)
    first = cut(dense)
    second = cut(dense - first)
    third = dense - first - second
    parts = jnp.concatenate([first, second, third], axis=1).astype(BF16)
    spare = -parts.shape[1] % 128
    parts = jnp.pad(parts, ((0, 0), (0, spare)))
    sent = jnp.concatenate([tokens, cotangent, parts], axis=1)
    held = lax.all_gather(sent, "expert", axis=0, tiled=True)
    tok = held[:, :width]
    cot = held[:, width : 2 * width]
    parts = held[:, 2 * width : 2 * width + 3 * expert_total].astype(F32)
    parts = parts.reshape(group, 3, expert_total)
    weight = parts[:, 0] + parts[:, 1] + parts[:, 2]
    weight = lax.dynamic_slice_in_dim(
        weight, lax.axis_index("expert") * expert_local, expert_local, axis=1
    ).T[:, :, None]
    share = width // n_dp

    def columns(shift):
        start = lax.rem(my_dp + shift, n_dp) * share
        return jnp.concatenate(
            [
                lax.dynamic_slice_in_dim(tok, start, share, axis=1),
                lax.dynamic_slice_in_dim(cot, start, share, axis=1),
            ],
            axis=1,
        )

    def moved(value, shift):
        return lax.ppermute(value, "dp", [(i, (i + shift) % n_dp) for i in range(n_dp)])

    sides = [columns(0)] + [moved(columns(s), s) for s in range(1, n_dp)]
    gate_up = jnp.einsum("td,edgh->etgh", tok, weights_gate_up, preferred_element_type=F32)
    gate_pre = gate_up[:, :, 0, :]
    up_pre = gate_up[:, :, 1, :]
    sig_gate = jax.nn.sigmoid(gate_pre)
    silu_gate = gate_pre * sig_gate
    hidden = (silu_gate * up_pre * weight).astype(BF16)
    hidden_grad = weight * jnp.einsum("td,edh->eth", cot, weights_down, preferred_element_type=F32)
    gate_grad = (hidden_grad * up_pre * sig_gate * (1.0 + gate_pre * (1.0 - sig_gate))).astype(BF16)
    up_grad = (hidden_grad * silu_gate).astype(BF16)
    mine = jnp.stack([gate_grad, up_grad, hidden], axis=0)
    acts = jnp.concatenate([mine] + [moved(mine, s) for s in range(1, n_dp)], axis=2)
    pre_grads = jnp.stack([gate_grad, up_grad], axis=2)
    out_part = jnp.sum(
        jnp.einsum("eth,edh->etd", hidden, weights_down, preferred_element_type=F32), axis=0
    ).astype(BF16)
    in_part = jnp.sum(
        jnp.einsum("etgh,edgh->etd", pre_grads, weights_gate_up, preferred_element_type=F32), axis=0
    ).astype(BF16)
    both = jnp.stack([out_part, in_part]).reshape(
        2, n_expert, tok_rows, n_tensor, width // n_tensor
    )
    both = both.transpose(1, 3, 0, 2, 4).reshape(
        n_expert * n_tensor, 2, tok_rows, width // n_tensor
    )
    back = lax.all_to_all(both, ("expert", "tensor"), split_axis=0, concat_axis=0, tiled=True)
    results = jnp.sum(back.astype(F32), axis=0).astype(BF16)
    rows = jnp.concatenate(sides, axis=0)
    gate_up_grad = jnp.einsum(
        "td,geth->edgh", rows[:, :share], acts[:2], preferred_element_type=F32
    ).astype(BF16)
    down_grad = jnp.einsum(
        "td,eth->edh", rows[:, share:], acts[2], preferred_element_type=F32
    ).astype(BF16)
    return (results[0], results[1], gate_up_grad, down_grad)


def solution(mesh):
    return jax.shard_map(
        body,
        mesh=mesh,
        in_specs=(
            P(("dp", "expert"), None),
            P(("dp", "expert"), None),
            P(("dp", "expert"), None),
            P("expert", None, None, "tensor"),
            P("expert", None, "tensor"),
            P(("dp", "expert"), None),
        ),
        out_specs=(
            P(("dp", "expert"), "tensor"),
            P(("dp", "expert"), "tensor"),
            P("expert", "dp", None, "tensor"),
            P("expert", "dp", "tensor"),
        ),
        check_vma=False,
    )
```

profile of v0, /device:TPU:0, one launch (start us, length us, event | category | flops | bytes accessed | tf_op | source)
XLA Modules:
  0.0 121.2 jit_solution(4500048296995259462)
XLA Ops:
  7.2 0.9 copy.62
  8.1 0.8 copy.63
  8.9 0.1 select_reduce_fusion
  9.1 1.5 %pad_maximum_fusion.4 = bf16[16,4224]{1,0:T(8,128)(2,1)} fusion(bf16[16,128]{1,0:T(8,128)(2,1)S(1)} %fusion.56, bf16[16,2048]{1,0:T(8,128)(2,1)} %param.11, bf16[16,2048]{1,0:T(8,128)(2,1)} %param.6), kind=kLoop, calls=%fused_computation.63 | loop fusion | flops 405504 | bytes 270336 | tf_op jit(solution)/shard_map/concatenate | solution.py:31
  10.7 25.1 %all-gather.2.cloned.1.call-done = bf16[128,4224]{1,0:T(8,128)(2,1)} async-done(((bf16[16,4224]{1,0:T(8,128)(2,1)}), bf16[128,4224]{1,0:T(8,128)(2,1)}) %all-gather.2.cloned.1.call-update) | async-done | bytes 1081360 | tf_op jit(solution)/shard_map/all_gather | solution.py:32
  35.8 0.8 slice.59
  36.7 4.0 %fusion.12 = f32[2,128,2,384]{3,1,2,0:T(8,128)S(1)} fusion(bf16[2,2048,2,384]{3,2,1,0:T(2,128)(2,1)} %param.9, bf16[128,4224]{1,0:T(8,128)(2,1)} %all-gather.2.cloned.1.call-done), kind=kOutput, calls=%fused_computation.11 | convolution fusion | flops 805306368 | bytes 7602176 | tf_op jit(solution)/shard_map/td,edgh->etgh/dot_general | solution.py:57
  40.7 0.9 copy-done.4
  41.5 2.0 %fusion.7 = bf16[128,2048]{1,0:T(8,128)(2,1)} fusion(bf16[2,2048,384]{2,1,0:T(8,128)(2,1)S(1)} %copy-done, f32[2,128,2,384]{3,1,2,0:T(8,128)S(1)} %fusion.12, f32[2,128]{1,0:T(2,128)S(1)} %fusion.58), kind=kOutput, calls=%fused_computation.7 | convolution fusion | flops 403603456 | bytes 4457472 | tf_op jit(solution)/shard_map/eth,edh->etd/dot_general | solution.py:70
  43.5 2.2 %stack.28 = bf16[1,8,16,2,1024]{4,3,2,1,0:T(2,128)(2,1)} reshape(bf16[128,2048]{1,0:T(8,128)(2,1)} %fusion.7) | data formatting | bytes 1048576 | tf_op jit(solution)/shard_map/stack | solution.py:75
  45.7 2.0 %copy.68 = bf16[1,8,16,2,1024]{4,2,0,3,1:T(8,128)(2,1)} copy(bf16[1,8,16,2,1024]{4,3,2,1,0:T(2,128)(2,1)} %stack.28) | data formatting | bytes 1048576 | tf_op jit(solution)/shard_map/stack | solution.py:75
  47.7 1.9 %fusion.44 = (bf16[2,128,384]{2,1,0:T(8,128)(2,1)S(1)}, bf16[2,128,384]{2,1,0:T(8,128)(2,1)S(1)}) fusion(f32[2,128,2,384]{3,1,2,0:T(8,128)} %copy-done.4, bf16[2,2048,384]{2,1,0:T(8,128)(2,1)S(1)} %copy-done, bf16[128,4224]{1,0:T(8,128)(2,1)} %all-gather.2.cloned.1.call-done, f32[2,128]{1,0:T(2,128)S(1)} %fusion.58), kind=kOutput, calls=%fused_computation.54 | convolution fusion | flops 404029440 | bytes 4850688 | tf_op jit(solution)/shard_map/td,edh->eth/dot_general | solution.py:63
  49.7 0.7 copy-done.2
  50.4 5.8 %fusion.8 = bf16[128,2048]{1,0:T(8,128)(2,1)} fusion(bf16[2,2048,2,384]{3,2,1,0:T(2,128)(2,1)} %param.9, bf16[2,128,1,384]{3,1,0,2:T(8,128)(2,1)S(1)} %bitcast.126, bf16[2,128,1,384]{3,1,0,2:T(8,128)(2,1)S(1)} %bitcast.122), kind=kOutput, calls=%fused_computation.8 | convolution fusion | flops 805765120 | bytes 7208960 | tf_op jit(solution)/shard_map/etgh,edgh->etd/dot_general | solution.py:73
  56.2 2.2 %stack.32 = bf16[1,8,16,2,1024]{4,3,2,1,0:T(2,128)(2,1)} reshape(bf16[128,2048]{1,0:T(8,128)(2,1)} %fusion.8) | data formatting | bytes 1048576 | tf_op jit(solution)/shard_map/stack | solution.py:75
  58.4 1.2 copy.69
  59.6 2.1 %pad_maximum_fusion = bf16[2,8,16,2,1024]{4,2,0,3,1:T(8,128)(2,1)} fusion(bf16[1,8,16,2,1024]{4,2,0,3,1:T(8,128)(2,1)S(1)} %copy.69, bf16[1,8,16,2,1024]{4,2,0,3,1:T(8,128)(2,1)} %copy.68), kind=kLoop, calls=%fused_computation.21 | loop fusion | flops 524288 | bytes 2097152 | tf_op jit(solution)/shard_map/stack | solution.py:75
  61.7 4.4 %all-to-all-start = ((bf16[16,2,16,1024]{3,2,1,0:T(8,128)(2,1)}), bf16[16,2,16,1024]{3,2,1,0:T(8,128)(2,1)}, u32[]{:S(2)}, u32[]{:S(2)}) async-start(bf16[16,2,16,1024]{3,2,1,0:T(8,128)(2,1)} %bitcast.121), calls=%async_computation | async-start | bytes 2097152 | tf_op jit(solution)/shard_map/all_to_all | solution.py:81
  66.2 1.3 %fusion.66 = (bf16[128,2048]{1,0:T(8,128)(2,1)S(1)}, bf16[128,2048]{1,0:T(8,128)(2,1)S(1)}) fusion(bf16[128,4224]{1,0:T(8,128)(2,1)} %all-gather.2.cloned.1.call-done), kind=kLoop, calls=%fused_computation.95 | loop fusion | bytes 2097152 | tf_op jit(solution)/shard_map/slice | solution.py:33
  67.5 0.1 constant_dynamic-slice_fusion.4
  67.7 1.5 %collective-permute-start.1 = (bf16[128,2048]{1,0:T(8,128)(2,1)S(1)}, bf16[128,2048]{1,0:T(8,128)(2,1)S(1)}, u32[]{:S(2)}, u32[]{:S(2)}) collective-permute-start(bf16[128,2048]{1,0:T(8,128)(2,1)S(1)} %pad_maximum_fusion.3), channel_id=1, source_target_pairs={{0,16},{16,0},{1,17},{17,1},{2,18},{18,2},{3,19},{19,3},{4,20},{20... | collective-permute-start | bytes 1572872 | tf_op jit(solution)/shard_map/ppermute | solution.py:54
  69.2 0.1 fusion.48
  69.4 0.6 collective-permute-start
  70.1 12.4 %collective-permute-done.1 = bf16[128,2048]{1,0:T(8,128)(2,1)S(1)} collective-permute-done((bf16[128,2048]{1,0:T(8,128)(2,1)S(1)}, bf16[128,2048]{1,0:T(8,128)(2,1)S(1)}, u32[]{:S(2)}, u32[]{:S(2)}) %collective-permute-start.1) | collective-permute-done | bytes 524320 | tf_op jit(solution)/shard_map/ppermute | solution.py:54
  82.6 12.0 %collective-permute-done = bf16[3,2,128,384]{3,2,1,0:T(8,128)(2,1)S(1)} collective-permute-done((bf16[3,2,128,384]{3,2,1,0:T(8,128)(2,1)S(1)}, bf16[3,2,128,384]{3,2,1,0:T(8,128)(2,1)S(1)}, u32[]{:S(2)}, u32[]{:S(2)}) %collective-permute-start) | collective-permute-done | bytes 589856 | tf_op jit(solution)/shard_map/ppermute | solution.py:54
  94.6 0.8 copy-done.6
  95.4 1.8 %fusion.11 = bf16[2,1024,384]{1,2,0:T(8,128)(2,1)} fusion(bf16[256,2048]{1,0:T(8,128)(2,1)S(1)} %pad_maximum_fusion.1, bf16[3,2,128,384]{3,2,1,0:T(8,128)(2,1)S(1)} %collective-permute-done, bf16[1,2,128,384]{3,2,1,0:T(8,128)(2,1)S(1)} %fusion.48, bf16[1,2,128,384]{3,2,1,0:T(8,128)(2,1)S(1)} %bitcast.129, bf16[1,2,128,384]{3,2,1,0:T(8,128)(2,1)S(1)} %bitcast.124), kind=kOutput, calls=%fused_computation.10 | convolution fusion | flops 405012480 | bytes 3276800 | tf_op jit(solution)/shard_map/td,eth->edh/dot_general | solution.py:87
  97.1 2.6 %copy.73 = bf16[2,1024,384]{2,1,0:T(8,128)(2,1)} copy(bf16[2,1024,384]{1,2,0:T(8,128)(2,1)} %fusion.11) | data formatting | bytes 3145728
  99.7 3.9 %convert_bitcast_fusion = bf16[2,1024,2,384]{1,3,0,2:T(8,128)(2,1)} fusion(bf16[3,2,128,384]{3,2,1,0:T(8,128)(2,1)} %copy-done.6, bf16[1,2,128,384]{3,2,1,0:T(8,128)(2,1)S(1)} %fusion.48, bf16[1,2,128,384]{3,2,1,0:T(8,128)(2,1)} %bitcast.127, bf16[1,2,128,384]{3,2,1,0:T(8,128)(2,1)S(1)} %bitcast.125, bf16[256,2048]{1,0:T(8,128)(2,1)} %copy-done.1), kind=kOutput, calls=%fused_computation.4 | convolution fusion | flops 811597824 | bytes 4849664 | tf_op jit(solution)/shard_map/td,geth->edgh/dot_general | solution.py:84
  103.6 8.7 %copy.72 = bf16[2,1024,2,384]{3,2,1,0:T(2,128)(2,1)} copy(bf16[2,1024,2,384]{1,3,0,2:T(8,128)(2,1)} %convert_bitcast_fusion) | data formatting | bytes 6291456
  112.3 1.4 %reduce_sum.23 = bf16[2,16,1024]{2,1,0:T(8,128)(2,1)S(1)} reduce(bf16[16,2,16,1024]{3,2,1,0:T(8,128)(2,1)} %all-to-all-done, bf16[]{:T(256)} %constant.23.clone.1), dimensions={0}, to_apply=%region_1.2 | reduce | flops 491520 | bytes 1114114 | tf_op jit(solution)/shard_map/reduce_sum | solution.py:82
  113.7 0.6 slice_bitcast_fusion.4
  (22 shorter events, 0.5 us)
Async XLA Ops:
  7.2 34.4 %copy-start = (bf16[2,2048,384]{2,1,0:T(8,128)(2,1)S(1)}, bf16[2,2048,384]{2,1,0:T(8,128)(2,1)}, u32[]{:S(2)}) copy-start(bf16[2,2048,384]{2,1,0:T(8,128)(2,1)} %param.10) | copy-start | bytes 9437188
  7.2 28.6 %all-gather.2.cloned.1.call-start = ((), (), s32[]{:S(2)}) async-start(), calls=%async_computation.1 | async-start | bytes 1216512 | tf_op jit(solution)/shard_map/all_gather | solution.py:32
  40.7 0.9 copy-start.4
  49.7 0.7 copy-start.2
  61.7 50.6 %all-to-all-start = ((bf16[16,2,16,1024]{3,2,1,0:T(8,128)(2,1)}), bf16[16,2,16,1024]{3,2,1,0:T(8,128)(2,1)}, u32[]{:S(2)}, u32[]{:S(2)}) async-start(bf16[16,2,16,1024]{3,2,1,0:T(8,128)(2,1)} %bitcast.121), calls=%async_computation | async-start | bytes 2097152 | tf_op jit(solution)/shard_map/all_to_all | solution.py:81
  66.1 3.0 %copy-start.5 = (f32[2,128,2,384]{3,1,2,0:T(8,128)S(1)}, f32[2,128,2,384]{3,1,2,0:T(8,128)}, u32[]{:S(2)}) copy-start(f32[2,128,2,384]{3,1,2,0:T(8,128)} %copy-done.4) | copy-start | bytes 2359300
  67.5 1.8 %copy-start.3 = (bf16[2,128,384]{2,1,0:T(8,128)(2,1)S(1)}, bf16[2,128,384]{2,1,0:T(8,128)(2,1)}, u32[]{:S(2)}) copy-start(bf16[2,128,384]{2,1,0:T(8,128)(2,1)} %copy-done.2) | copy-start | bytes 589828
  67.7 14.8 %collective-permute-start.1 = (bf16[128,2048]{1,0:T(8,128)(2,1)S(1)}, bf16[128,2048]{1,0:T(8,128)(2,1)S(1)}, u32[]{:S(2)}, u32[]{:S(2)}) collective-permute-start(bf16[128,2048]{1,0:T(8,128)(2,1)S(1)} %pad_maximum_fusion.3), channel_id=1, source_target_pairs={{0,16},{16,0},{1,17},{17,1},{2,18},{18,2},{3,19},{19,3},{4,20},{20... | collective-permute-start | bytes 1572872 | tf_op jit(solution)/shard_map/ppermute | solution.py:54
  69.4 25.1 %collective-permute-start = (bf16[3,2,128,384]{3,2,1,0:T(8,128)(2,1)S(1)}, bf16[3,2,128,384]{3,2,1,0:T(8,128)(2,1)S(1)}, u32[]{:S(2)}, u32[]{:S(2)}) collective-permute-start(bf16[3,2,128,384]{3,2,1,0:T(8,128)(2,1)S(1)} %pad_maximum_fusion.2), channel_id=1, source_target_pairs={{0,16},{16,0},{1,17},{17,1},{2,18},{18,2},{3,19},{19,3},{4,20},{20... | collective-permute-start | bytes 1769480 | tf_op jit(solution)/shard_map/ppermute | solution.py:54
  82.6 12.0 %copy-start.1 = (bf16[256,2048]{1,0:T(8,128)(2,1)}, bf16[256,2048]{1,0:T(8,128)(2,1)S(1)}, u32[]{:S(2)}) copy-start(bf16[256,2048]{1,0:T(8,128)(2,1)S(1)} %pad_maximum_fusion.1) | copy-start | bytes 3145732
  94.6 0.8 copy-start.6
Sparse Core Ops, SparseCore 0:
  10.8 24.9 all-gather.1
where the time goes:
time: 122 us; the launch traced here: 121 us
  waiting for transfers between devices  49.5 us (41%)
  local copies, waits for them, and re-layouts  25.9 us (21%)
  matrix products  19.3 us (16%)
  between operations  14.2 us (12%)
  starting transfers between devices  6.63 us (5%)
  other arithmetic  5.65 us (5%)
    all_gather x1, waiting for transfers between devices, body(): held = lax.all_gather(sent, 'expert', axis=0, tiled=True)  25.1 us
    ppermute x2, waiting for transfers between devices, moved(): lax.ppermute(value, 'dp', [(i, (i + shift) % n_dp) for i in range(n_dp)])  24.4 us
    unnamed x19, local copies, waits for them, and re-layouts  15.4 us
    another operation x4, local copies, waits for them, and re-layouts, body(): jnp.stack([out_part, in_part])  7.64 us
    dot_general x1, matrix products, body(): jnp.einsum('etgh,edgh->etd', pre_grads, weights_gate_up, preferred_elemen...  5.78 us
    all_to_all x1, starting transfers between devices, body(): lax.all_to_all(both, ('expert', 'tensor'), split_axis=0, concat_axis=0, t...  4.42 us
    dot_general x1, matrix products, body(): jnp.einsum('td,edgh->etgh', tok, weights_gate_up, preferred_element_type=...  3.95 us
    dot_general x1, matrix products, body(): jnp.einsum('td,geth->edgh', rows[:, :share], acts[:2], preferred_element_...  3.9 us
  transfers between devices with their start and end apart: 4, of which 3 were waited for; matrix products, arithmetic and copies ran while one was open for 15% of the time, Pallas kernels for 0%

commit v1 on v0

--- a/solution.py
+++ b/solution.py
@@ -29,7 +29,21 @@
     spare = -parts.shape[1] % 128
     parts = jnp.pad(parts, ((0, 0), (0, spare)))
     sent = jnp.concatenate([tokens, cotangent, parts], axis=1)
-    held = lax.all_gather(sent, "expert", axis=0, tiled=True)
+    ways, here, lap = (lax.axis_size("expert"), lax.axis_index("expert"), sent.shape[0])
+    dims = [n * ways if d == 0 else n for d, n in enumerate(sent.shape)]
+    full = lax.dynamic_update_slice_in_dim(jnp.zeros(dims, sent.dtype), sent, here * lap, axis=0)
+    going_up = going_down = sent
+    for far in range(1, ways // 2 + 1):
+        going_up = lax.ppermute(going_up, "expert", [(d, (d + 1) % ways) for d in range(ways)])
+        full = lax.dynamic_update_slice_in_dim(full, going_up, (here - far) % ways * lap, axis=0)
+        if 2 * far < ways:
+            going_down = lax.ppermute(
+                going_down, "expert", [(d, (d - 1) % ways) for d in range(ways)]
+            )
+            full = lax.dynamic_update_slice_in_dim(
+                full, going_down, (here + far) % ways * lap, axis=0
+            )
+    held = full
     tok = held[:, :width]
     cot = held[:, width : 2 * width]
     parts = held[:, 2 * width : 2 * width + 3 * expert_total].astype(F32)

time: 122 us -> 220 us (1.80); the launches traced: 121 us -> 216 us
  local copies, waits for them, and re-layouts: 25.9 us -> 139 us
  waiting for transfers between devices: 49.5 us -> 33 us
  starting transfers between devices: 6.63 us -> 21.1 us
  between operations: 14.2 us -> 0.86 us
  matrix products: 19.3 us -> 16.7 us
    dynamic_update_slice x0 -> x8, local copies, waits for them, and re-layouts: none -> 100 us  [the longest x4 51 us: body(): lax.dynamic_update_slice_in_dim(full, going_up, (here - far) % ways * lap...]
    all_gather x1 -> x0, waiting for transfers between devices: 25.1 us -> none  [body(): held = lax.all_gather(sent, 'expert', axis=0, tiled=True)]
    ppermute x0 -> x7, local copies, waits for them, and re-layouts: none -> 12.3 us  [the longest x4 7.29 us: body(): lax.ppermute(going_up, 'expert', [(d, (d + 1) % ways) for d in range(ways)])]
    ppermute x0 -> x7, starting transfers between devices: none -> 11.9 us  [the longest x3 11.3 us: body(): lax.ppermute(going_down, 'expert', [(d, (d - 1) % ways) for d in range(wa...]
    ppermute x0 -> x7, waiting for transfers between devices: none -> 9.04 us  [the longest x4 8.96 us: body(): lax.ppermute(going_up, 'expert', [(d, (d + 1) % ways) for d in range(ways)])]
    dot_general x1, matrix products: 5.78 us -> 3.02 us  [body(): jnp.einsum('etgh,edgh->etd', pre_grads, weights_gate_up, preferred_elemen...]
    all_to_all x1, starting transfers between devices: 4.42 us -> 6.74 us  [body(): lax.all_to_all(both, ('expert', 'tensor'), split_axis=0, concat_axis=0, t...]
    unnamed x19 -> x32, local copies, waits for them, and re-layouts: 15.4 us -> 13.9 us
  transfers between devices with their start and end apart: 4 -> 10, of which waited for: 3 -> 6; matrix products, arithmetic and copies ran while one was open for 15% -> 55% of each run, Pallas kernels for 0% -> 0%
where the time goes in v1:
time: 220 us; the launch traced here: 216 us
  local copies, waits for them, and re-layouts  139 us (63%)
  waiting for transfers between devices  33 us (15%)
  starting transfers between devices  21.1 us (10%)
  matrix products  16.7 us (8%)
  other arithmetic  4.99 us (2%)
    dynamic_update_slice x4, local copies, waits for them, and re-layouts, body(): lax.dynamic_update_slice_in_dim(full, going_up, (here - far) % ways * lap...  51 us
    dynamic_update_slice x3, local copies, waits for them, and re-layouts, body(): lax.dynamic_update_slice_in_dim(full, going_down, (here + far) % ways * l...  38.3 us
    ppermute x2, waiting for transfers between devices, moved(): lax.ppermute(value, 'dp', [(i, (i + shift) % n_dp) for i in range(n_dp)])  24 us
    unnamed x32, local copies, waits for them, and re-layouts  13.9 us
    ppermute x3, starting transfers between devices, body(): lax.ppermute(going_down, 'expert', [(d, (d - 1) % ways) for d in range(wa...  11.3 us
    dynamic_update_slice x1, local copies, waits for them, and re-layouts, body(): lax.dynamic_update_slice_in_dim(jnp.zeros(dims, sent.dtype), sent, here *...  10.9 us
    ppermute x4, waiting for transfers between devices, body(): lax.ppermute(going_up, 'expert', [(d, (d + 1) % ways) for d in range(ways)])  8.96 us
    another operation x4, local copies, waits for them, and re-layouts, body(): jnp.stack([out_part, in_part])  7.58 us
  transfers between devices with their start and end apart: 10, of which 6 were waited for; matrix products, arithmetic and copies ran while one was open for 55% of the time, Pallas kernels for 0%

profile of v1, /device:TPU:0, one launch (start us, length us, event | category | flops | bytes accessed | tf_op | source)
XLA Modules:
  0.0 215.7 jit_solution(3481987651661811042)
XLA Ops:
  4.0 4.1 %collective-permute-start.1 = (bf16[16,4224]{1,0:T(8,128)(2,1)S(1)}, bf16[16,4224]{1,0:T(8,128)(2,1)S(1)}, u32[]{:S(2)}, u32[]{:S(2)}) collective-permute-start(bf16[16,4224]{1,0:T(8,128)(2,1)S(1)} %pad_maximum_fusion.4), channel_id=1, source_target_pairs={{0,14},{2,0},{4,2},{6,4},{8,6},{10,8},{12,10},{14,12},{1,15},{3,1}... | collective-permute-start | bytes 405512 | tf_op jit(solution)/shard_map/ppermute | solution.py:40
  8.1 2.7 %collective-permute-done = bf16[16,4224]{1,0:T(8,128)(2,1)S(1)} collective-permute-done((bf16[16,4224]{1,0:T(8,128)(2,1)S(1)}, bf16[16,4224]{1,0:T(8,128)(2,1)S(1)}, u32[]{:S(2)}, u32[]{:S(2)}) %collective-permute-start) | collective-permute-done | bytes 135200 | tf_op jit(solution)/shard_map/ppermute | solution.py:37
  10.8 3.5 %collective-permute-start.3 = (bf16[16,4224]{1,0:T(8,128)(2,1)S(1)}, bf16[16,4224]{1,0:T(8,128)(2,1)S(1)}, u32[]{:S(2)}, u32[]{:S(2)}) collective-permute-start(bf16[16,4224]{1,0:T(8,128)(2,1)S(1)} %collective-permute-done.1), channel_id=1, source_target_pairs={{0,14},{2,0},{4,2},{6,4},{8,6},{10,8},{12,10},{14,12},{1,15},{3,1}... | collective-permute-start | bytes 405512 | tf_op jit(solution)/shard_map/ppermute | solution.py:40
  14.3 3.5 %collective-permute-done.2 = bf16[16,4224]{1,0:T(8,128)(2,1)S(1)} collective-permute-done((bf16[16,4224]{1,0:T(8,128)(2,1)S(1)}, bf16[16,4224]{1,0:T(8,128)(2,1)S(1)}, u32[]{:S(2)}, u32[]{:S(2)}) %collective-permute-start.2) | collective-permute-done | bytes 135200 | tf_op jit(solution)/shard_map/ppermute | solution.py:37
  17.9 3.7 %collective-permute-start.5 = (bf16[16,4224]{1,0:T(8,128)(2,1)S(1)}, bf16[16,4224]{1,0:T(8,128)(2,1)}, u32[]{:S(2)}, u32[]{:S(2)}) collective-permute-start(bf16[16,4224]{1,0:T(8,128)(2,1)S(1)} %collective-permute-done.3), channel_id=1, source_target_pairs={{0,14},{2,0},{4,2},{6,4},{8,6},{10,8},{12,10},{14,12},{1,15},{3,1}... | collective-permute-start | bytes 405512 | tf_op jit(solution)/shard_map/ppermute | solution.py:40
  21.6 2.8 %collective-permute-done.4 = bf16[16,4224]{1,0:T(8,128)(2,1)S(1)} collective-permute-done((bf16[16,4224]{1,0:T(8,128)(2,1)S(1)}, bf16[16,4224]{1,0:T(8,128)(2,1)S(1)}, u32[]{:S(2)}, u32[]{:S(2)}) %collective-permute-start.4) | collective-permute-done | bytes 135200 | tf_op jit(solution)/shard_map/ppermute | solution.py:37
  26.9 10.9 %dynamic_update_slice.24 = bf16[128,4224]{0,1:T(8,128)(2,1)} dynamic-update-slice(bf16[128,4224]{0,1:T(8,128)(2,1)} %broadcast_in_dim.19, bf16[16,4224]{0,1:T(8,128)(2,1)} %copy.64, s32[]{:T(128)S(6)} %select_n.71, s32[]{:T(128)} %constant.69.clone.1) | dynamic-update-slice | bytes 270340 | tf_op jit(solution)/shard_map/dynamic_update_slice | solution.py:34
  37.7 2.3 %copy.65 = bf16[16,4224]{0,1:T(8,128)(2,1)} copy(bf16[16,4224]{1,0:T(8,128)(2,1)} %copy-done.11) | data formatting | bytes 270336 | tf_op jit(solution)/shard_map/ppermute | solution.py:37
  40.0 12.7 %dynamic_update_slice.25 = bf16[128,4224]{0,1:T(8,128)(2,1)} dynamic-update-slice(bf16[128,4224]{0,1:T(8,128)(2,1)} %dynamic_update_slice.24, bf16[16,4224]{0,1:T(8,128)(2,1)} %copy.65, s32[]{:T(128)S(6)} %select_n.73, s32[]{:T(128)} %constant.69.clone.1) | dynamic-update-slice | bytes 270340 | tf_op jit(solution)/shard_map/dynamic_update_slice | solution.py:38
  54.1 12.8 %dynamic_update_slice.26 = bf16[128,4224]{0,1:T(8,128)(2,1)} dynamic-update-slice(bf16[128,4224]{0,1:T(8,128)(2,1)} %dynamic_update_slice.25, bf16[16,4224]{0,1:T(8,128)(2,1)} %copy.66, s32[]{:T(128)S(6)} %select_n.75, s32[]{:T(128)} %constant.69.clone.1) | dynamic-update-slice | bytes 270340 | tf_op jit(solution)/shard_map/dynamic_update_slice | solution.py:43
  68.3 12.7 %dynamic_update_slice.27 = bf16[128,4224]{0,1:T(8,128)(2,1)} dynamic-update-slice(bf16[128,4224]{0,1:T(8,128)(2,1)} %dynamic_update_slice.26, bf16[16,4224]{0,1:T(8,128)(2,1)} %copy.67, s32[]{:T(128)S(6)} %select_n.77, s32[]{:T(128)} %constant.69.clone.1) | dynamic-update-slice | bytes 270340 | tf_op jit(solution)/shard_map/dynamic_update_slice | solution.py:38
  82.4 12.7 %dynamic_update_slice.28 = bf16[128,4224]{0,1:T(8,128)(2,1)} dynamic-update-slice(bf16[128,4224]{0,1:T(8,128)(2,1)} %dynamic_update_slice.27, bf16[16,4224]{0,1:T(8,128)(2,1)} %copy.68, s32[]{:T(128)S(6)} %select_n.79, s32[]{:T(128)} %constant.69.clone.1) | dynamic-update-slice | bytes 270340 | tf_op jit(solution)/shard_map/dynamic_update_slice | solution.py:43
  96.5 12.7 %dynamic_update_slice.29 = bf16[128,4224]{0,1:T(8,128)(2,1)} dynamic-update-slice(bf16[128,4224]{0,1:T(8,128)(2,1)} %dynamic_update_slice.28, bf16[16,4224]{0,1:T(8,128)(2,1)} %copy.69, s32[]{:T(128)S(6)} %select_n.81, s32[]{:T(128)} %constant.69.clone.1) | dynamic-update-slice | bytes 270340 | tf_op jit(solution)/shard_map/dynamic_update_slice | solution.py:38
  109.2 2.3 %copy.70 = bf16[16,4224]{0,1:T(8,128)(2,1)} copy(bf16[16,4224]{1,0:T(8,128)(2,1)} %collective-permute-done.5) | data formatting | bytes 270336 | tf_op jit(solution)/shard_map/ppermute | solution.py:40
  111.5 12.7 %dynamic_update_slice.30 = bf16[128,4224]{0,1:T(8,128)(2,1)} dynamic-update-slice(bf16[128,4224]{0,1:T(8,128)(2,1)} %dynamic_update_slice.29, bf16[16,4224]{0,1:T(8,128)(2,1)} %copy.70, s32[]{:T(128)S(6)} %select_n.83, s32[]{:T(128)} %constant.69.clone.1) | dynamic-update-slice | bytes 270340 | tf_op jit(solution)/shard_map/dynamic_update_slice | solution.py:43
  124.2 2.3 %copy.71 = bf16[16,4224]{0,1:T(8,128)(2,1)} copy(bf16[16,4224]{1,0:T(8,128)(2,1)} %collective-permute-done.6) | data formatting | bytes 270336 | tf_op jit(solution)/shard_map/ppermute | solution.py:37
  126.5 12.7 %dynamic_update_slice.31 = bf16[128,4224]{0,1:T(8,128)(2,1)} dynamic-update-slice(bf16[128,4224]{0,1:T(8,128)(2,1)} %dynamic_update_slice.30, bf16[16,4224]{0,1:T(8,128)(2,1)} %copy.71, s32[]{:T(128)S(6)} %select_n.85, s32[]{:T(128)} %constant.69.clone.1) | dynamic-update-slice | bytes 270340 | tf_op jit(solution)/shard_map/dynamic_update_slice | solution.py:38
  139.9 4.1 %fusion.12 = f32[2,128,2,384]{3,1,2,0:T(8,128)S(1)} fusion(bf16[2,2048,2,384]{3,2,1,0:T(2,128)(2,1)} %param.9, bf16[128,4224]{0,1:T(8,128)(2,1)} %dynamic_update_slice.31), kind=kOutput, calls=%fused_computation.11 | convolution fusion | flops 805306368 | bytes 7602176 | tf_op jit(solution)/shard_map/td,edgh->etgh/dot_general | solution.py:71
  144.1 2.0 fusion.44
  146.2 2.0 fusion.7
  148.1 3.0 %fusion.8 = bf16[128,2048]{1,0:T(8,128)(2,1)} fusion(bf16[2,2048,2,384]{3,2,1,0:T(2,128)(2,1)S(1)} %bitcast.128, bf16[2,128,1,384]{3,1,0,2:T(8,128)(2,1)S(1)} %bitcast.122, bf16[2,128,1,384]{3,1,0,2:T(8,128)(2,1)S(1)} %bitcast.118), kind=kOutput, calls=%fused_computation.8 | convolution fusion | flops 805765120 | bytes 7208960 | tf_op jit(solution)/shard_map/etgh,edgh->etd/dot_general | solution.py:87
  151.2 2.2 %stack.32 = bf16[1,8,16,2,1024]{4,3,2,1,0:T(2,128)(2,1)} reshape(bf16[128,2048]{1,0:T(8,128)(2,1)} %fusion.8) | data formatting | bytes 1048576 | tf_op jit(solution)/shard_map/stack | solution.py:89
  153.4 2.0 copy.78
  155.4 2.2 %stack.28 = bf16[1,8,16,2,1024]{4,3,2,1,0:T(2,128)(2,1)} reshape(bf16[128,2048]{1,0:T(8,128)(2,1)} %fusion.7) | data formatting | bytes 1048576 | tf_op jit(solution)/shard_map/stack | solution.py:89
  158.7 2.1 pad_maximum_fusion
  160.9 6.7 %all-to-all-start = ((bf16[16,2,16,1024]{3,2,1,0:T(8,128)(2,1)}), bf16[16,2,16,1024]{3,2,1,0:T(8,128)(2,1)}, u32[]{:S(2)}, u32[]{:S(2)}) async-start(bf16[16,2,16,1024]{3,2,1,0:T(8,128)(2,1)} %bitcast.117), calls=%async_computation | async-start | bytes 2097152 | tf_op jit(solution)/shard_map/all_to_all | solution.py:95
  171.8 12.0 %collective-permute-done.8 = bf16[128,2048]{0,1:T(8,128)(2,1)S(1)} collective-permute-done((bf16[128,2048]{0,1:T(8,128)(2,1)S(1)}, bf16[128,2048]{0,1:T(8,128)(2,1)S(1)}, u32[]{:S(2)}, u32[]{:S(2)}) %collective-permute-start.8) | collective-permute-done | bytes 524320 | tf_op jit(solution)/shard_map/ppermute | solution.py:68
  184.0 11.9 %collective-permute-done.7 = bf16[3,2,128,384]{3,2,1,0:T(8,128)(2,1)S(1)} collective-permute-done((bf16[3,2,128,384]{3,2,1,0:T(8,128)(2,1)S(1)}, bf16[3,2,128,384]{3,2,1,0:T(8,128)(2,1)S(1)}, u32[]{:S(2)}, u32[]{:S(2)}) %collective-permute-start.7) | collective-permute-done | bytes 589856 | tf_op jit(solution)/shard_map/ppermute | solution.py:68
  196.8 2.7 %convert_bitcast_fusion = bf16[2,1024,2,384]{1,3,0,2:T(8,128)(2,1)} fusion(bf16[3,2,128,384]{3,2,1,0:T(8,128)(2,1)S(1)} %collective-permute-done.7, bf16[1,2,128,384]{3,2,1,0:T(8,128)(2,1)S(1)} %fusion.48, bf16[1,2,128,384]{3,2,1,0:T(8,128)(2,1)S(1)} %bitcast.125, bf16[1,2,128,384]{3,2,1,0:T(8,128)(2,1)S(1)} %bitcast.120, ...), kind=kOutput, calls=%fused_computation.4 | convolution fusion | flops 811597824 | bytes 4849664 | tf_op jit(solution)/shard_map/td,geth->edgh/dot_general | solution.py:98
  199.4 8.7 %copy.83 = bf16[2,1024,2,384]{3,2,1,0:T(2,128)(2,1)} copy(bf16[2,1024,2,384]{1,3,0,2:T(8,128)(2,1)} %convert_bitcast_fusion) | data formatting | bytes 6291456
  208.1 3.0 %fusion.11 = bf16[2,1024,384]{1,2,0:T(8,128)(2,1)} fusion(bf16[256,2048]{0,1:T(8,128)(2,1)} %copy-done.1, bf16[3,2,128,384]{3,2,1,0:T(8,128)(2,1)} %copy-done.6, bf16[1,2,128,384]{3,2,1,0:T(8,128)(2,1)S(1)} %fusion.48, bf16[1,2,128,384]{3,2,1,0:T(8,128)(2,1)} %bitcast.123, bf16[1,2,128,384]{3,2,1,0:T(8,128)(2,1)S(1)} %bitcast.121), kind=kOutput, calls=%fused_computation.10 | convolution fusion | flops 405012480 | bytes 3276800 | tf_op jit(solution)/shard_map/td,eth->edh/dot_general | solution.py:101
  211.1 2.6 %copy.84 = bf16[2,1024,384]{2,1,0:T(8,128)(2,1)} copy(bf16[2,1024,384]{1,2,0:T(8,128)(2,1)} %fusion.11) | data formatting | bytes 3145728
  (64 shorter events, 20.4 us)
Async XLA Ops:
  0.6 143.5 %copy-start = (bf16[2,2048,384]{2,1,0:T(8,128)(2,1)S(1)}, bf16[2,2048,384]{2,1,0:T(8,128)(2,1)}, u32[]{:S(2)}) copy-start(bf16[2,2048,384]{2,1,0:T(8,128)(2,1)} %param.10) | copy-start | bytes 9437188
  3.5 7.3 %collective-permute-start = (bf16[16,4224]{1,0:T(8,128)(2,1)S(1)}, bf16[16,4224]{1,0:T(8,128)(2,1)S(1)}, u32[]{:S(2)}, u32[]{:S(2)}) collective-permute-start(bf16[16,4224]{1,0:T(8,128)(2,1)S(1)} %pad_maximum_fusion.4), channel_id=1, source_target_pairs={{0,2},{2,4},{4,6},{6,8},{8,10},{10,12},{12,14},{14,0},{1,3},{3,5},... | collective-permute-start | bytes 405512 | tf_op jit(solution)/shard_map/ppermute | solution.py:37
  4.0 6.8 %collective-permute-start.1 = (bf16[16,4224]{1,0:T(8,128)(2,1)S(1)}, bf16[16,4224]{1,0:T(8,128)(2,1)S(1)}, u32[]{:S(2)}, u32[]{:S(2)}) collective-permute-start(bf16[16,4224]{1,0:T(8,128)(2,1)S(1)} %pad_maximum_fusion.4), channel_id=1, source_target_pairs={{0,14},{2,0},{4,2},{6,4},{8,6},{10,8},{12,10},{14,12},{1,15},{3,1}... | collective-permute-start | bytes 405512 | tf_op jit(solution)/shard_map/ppermute | solution.py:40
  10.8 3.6 %copy-start.11 = (bf16[16,4224]{1,0:T(8,128)(2,1)}, bf16[16,4224]{1,0:T(8,128)(2,1)S(1)}, u32[]{:S(2)}) copy-start(bf16[16,4224]{1,0:T(8,128)(2,1)S(1)} %collective-permute-done) | copy-start | bytes 405508
  10.8 7.0 %collective-permute-start.2 = (bf16[16,4224]{1,0:T(8,128)(2,1)S(1)}, bf16[16,4224]{1,0:T(8,128)(2,1)S(1)}, u32[]{:S(2)}, u32[]{:S(2)}) collective-permute-start(bf16[16,4224]{1,0:T(8,128)(2,1)S(1)} %collective-permute-done), channel_id=1, source_target_pairs={{0,2},{2,4},{4,6},{6,8},{8,10},{10,12},{12,14},{14,0},{1,3},{3,5},... | collective-permute-start | bytes 405512 | tf_op jit(solution)/shard_map/ppermute | solution.py:37
  10.8 13.6 %copy-start.7 = (bf16[16,4224]{1,0:T(8,128)(2,1)}, bf16[16,4224]{1,0:T(8,128)(2,1)S(1)}, u32[]{:S(2)}) copy-start(bf16[16,4224]{1,0:T(8,128)(2,1)S(1)} %collective-permute-done.1) | copy-start | bytes 405508
  10.8 7.1 %collective-permute-start.3 = (bf16[16,4224]{1,0:T(8,128)(2,1)S(1)}, bf16[16,4224]{1,0:T(8,128)(2,1)S(1)}, u32[]{:S(2)}, u32[]{:S(2)}) collective-permute-start(bf16[16,4224]{1,0:T(8,128)(2,1)S(1)} %collective-permute-done.1), channel_id=1, source_target_pairs={{0,14},{2,0},{4,2},{6,4},{8,6},{10,8},{12,10},{14,12},{1,15},{3,1}... | collective-permute-start | bytes 405512 | tf_op jit(solution)/shard_map/ppermute | solution.py:40
  17.8 6.6 %copy-start.9 = (bf16[16,4224]{1,0:T(8,128)(2,1)}, bf16[16,4224]{1,0:T(8,128)(2,1)S(1)}, u32[]{:S(2)}) copy-start(bf16[16,4224]{1,0:T(8,128)(2,1)S(1)} %collective-permute-done.2) | copy-start | bytes 405508
  17.8 6.5 %collective-permute-start.4 = (bf16[16,4224]{1,0:T(8,128)(2,1)S(1)}, bf16[16,4224]{1,0:T(8,128)(2,1)S(1)}, u32[]{:S(2)}, u32[]{:S(2)}) collective-permute-start(bf16[16,4224]{1,0:T(8,128)(2,1)S(1)} %collective-permute-done.2), channel_id=1, source_target_pairs={{0,2},{2,4},{4,6},{6,8},{8,10},{10,12},{12,14},{14,0},{1,3},{3,5},... | collective-permute-start | bytes 405512 | tf_op jit(solution)/shard_map/ppermute | solution.py:37
  17.9 91.3 %collective-permute-start.5 = (bf16[16,4224]{1,0:T(8,128)(2,1)S(1)}, bf16[16,4224]{1,0:T(8,128)(2,1)}, u32[]{:S(2)}, u32[]{:S(2)}) collective-permute-start(bf16[16,4224]{1,0:T(8,128)(2,1)S(1)} %collective-permute-done.3), channel_id=1, source_target_pairs={{0,14},{2,0},{4,2},{6,4},{8,6},{10,8},{12,10},{14,12},{1,15},{3,1}... | collective-permute-start | bytes 405512 | tf_op jit(solution)/shard_map/ppermute | solution.py:40
  24.4 99.9 %collective-permute-start.6 = (bf16[16,4224]{1,0:T(8,128)(2,1)S(1)}, bf16[16,4224]{1,0:T(8,128)(2,1)}, u32[]{:S(2)}, u32[]{:S(2)}) collective-permute-start(bf16[16,4224]{1,0:T(8,128)(2,1)S(1)} %collective-permute-done.4), channel_id=1, source_target_pairs={{0,2},{2,4},{4,6},{6,8},{8,10},{10,12},{12,14},{14,0},{1,3},{3,5},... | collective-permute-start | bytes 405512 | tf_op jit(solution)/shard_map/ppermute | solution.py:37
  37.7 15.0 %copy-start.8 = (bf16[16,4224]{1,0:T(8,128)(2,1)S(1)}, bf16[16,4224]{1,0:T(8,128)(2,1)}, u32[]{:S(2)}) copy-start(bf16[16,4224]{1,0:T(8,128)(2,1)} %copy-done.7) | copy-start | bytes 405508
  54.1 12.8 %copy-start.10 = (bf16[16,4224]{1,0:T(8,128)(2,1)S(1)}, bf16[16,4224]{1,0:T(8,128)(2,1)}, u32[]{:S(2)}) copy-start(bf16[16,4224]{1,0:T(8,128)(2,1)} %copy-done.9) | copy-start | bytes 405508
  139.9 8.2 %slice-start = ((s8[6291456]{0:T(1024)(128)(4,1)}), s8[4194304]{0:T(1024)(128)(4,1)S(1)}, s32[]{:S(2)}) async-start(s8[6291456]{0:T(1024)(128)(4,1)} %bitcast.127), calls=%async_computation.1 | async-start | bytes 8388608
  144.0 2.1 copy-start.4
  144.1 4.0 %slice-start.1 = ((s8[6291456]{0:T(1024)(128)(4,1)}), s8[2097152]{0:T(1024)(128)(4,1)S(1)}, s32[]{:S(2)}) async-start(s8[6291456]{0:T(1024)(128)(4,1)} %bitcast.127), calls=%async_computation.2 | async-start | bytes 4194304
  146.2 2.0 copy-start.2
  160.9 52.8 %all-to-all-start = ((bf16[16,2,16,1024]{3,2,1,0:T(8,128)(2,1)}), bf16[16,2,16,1024]{3,2,1,0:T(8,128)(2,1)}, u32[]{:S(2)}, u32[]{:S(2)}) async-start(bf16[16,2,16,1024]{3,2,1,0:T(8,128)(2,1)} %bitcast.117), calls=%async_computation | async-start | bytes 2097152 | tf_op jit(solution)/shard_map/all_to_all | solution.py:95
  168.9 1.7 copy-start.5
  168.9 1.8 copy-start.3
  169.0 14.8 %collective-permute-start.8 = (bf16[128,2048]{0,1:T(8,128)(2,1)S(1)}, bf16[128,2048]{0,1:T(8,128)(2,1)S(1)}, u32[]{:S(2)}, u32[]{:S(2)}) collective-permute-start(bf16[128,2048]{0,1:T(8,128)(2,1)S(1)} %pad_maximum_fusion.3), channel_id=1, source_target_pairs={{0,16},{16,0},{1,17},{17,1},{2,18},{18,2},{3,19},{19,3},{4,20},{20... | collective-permute-start | bytes 1572872 | tf_op jit(solution)/shard_map/ppermute | solution.py:68
  170.8 25.1 %collective-permute-start.7 = (bf16[3,2,128,384]{3,2,1,0:T(8,128)(2,1)S(1)}, bf16[3,2,128,384]{3,2,1,0:T(8,128)(2,1)S(1)}, u32[]{:S(2)}, u32[]{:S(2)}) collective-permute-start(bf16[3,2,128,384]{3,2,1,0:T(8,128)(2,1)S(1)} %pad_maximum_fusion.2), channel_id=1, source_target_pairs={{0,16},{16,0},{1,17},{17,1},{2,18},{18,2},{3,19},{19,3},{4,20},{20... | collective-permute-start | bytes 1769480 | tf_op jit(solution)/shard_map/ppermute | solution.py:68
  184.0 12.0 %copy-start.1 = (bf16[256,2048]{0,1:T(8,128)(2,1)}, bf16[256,2048]{0,1:T(8,128)(2,1)S(1)}, u32[]{:S(2)}) copy-start(bf16[256,2048]{0,1:T(8,128)(2,1)S(1)} %pad_maximum_fusion.1) | copy-start | bytes 3145732
  195.9 0.8 copy-start.6
